TPU v7x, 32 devices: a whole 2x2x4 slice. The times are simulated.
32 devices in a mesh: video: 2 (over x), frame: 4 (over z), head: 4 (over y, core).
Axes of the slice: x: 2, y: 2, z: 4, core: 2. Of those that a mesh axis runs over, the one named last changes fastest.
Arguments:
- latents: bfloat16 [2048, 2560], P(('video', 'frame', 'head')), parts along dimension 0, may hold values from -24 to 24
- weights: bfloat16 [2560, 3, 2560], P(None, None, 'head'), may hold values from -0.125 to 0.125
- key_slots: int32 [16, 4, 4], P('frame'), may hold values from 0 to 3, as said below
- key_count: int32 [16, 4], P('frame'), may hold values from 0 to 4, as said below
Outputs:
- attended: bfloat16 [2048, 2560], P(('video', 'frame'), 'head'), parts along dimension 0
There are 2 independent parts, one for each index of `video`. A program takes and returns all parts, laid end to end along the dimension named above; an argument that names none is the same for every part. Nothing has to cross between parts.
Inputs may be any that keep to these rules, and one draw needn't show every extreme that they name: key_slots[a, b, :] is a permutation of the local block numbers of a slab. key_count[a, b] is 4 when query block a lies in slab b; otherwise it is at most max(1, 4 // p), where p is the largest power of two not above the distance between a's slab and b.
All inputs are finite; a program needn't handle non-finite values.
Results may differ from a plain program's by a relative error of at most 0.012.
The roundings to bfloat16 on the way count: a program that leaves them out, or rounds other values in their place, can miss the bound.
Values may be sent and summed in bfloat16 or wider, within the bound.
A program may use at most 128 MiB of HBM per device.

v0:
```python
import jax
import jax.numpy as jnp
from jax import lax
from jax.sharding import PartitionSpec as P

HD = 128


masked_score = -1e30


def on_device(latents, weights, key_slots, key_count):
    width_in = weights.shape[0]
    local_width = weights.shape[2]
    w_joined = weights.reshape(width_in, 3 * local_width)
    joined = jnp.dot(
        lax.all_gather(latents, "head", axis=0, tiled=True),
        w_joined,
        preferred_element_type=jnp.float32,
    ).astype(jnp.bfloat16)
    slab_len = joined.shape[0]
    head_count = local_width // HD
    query_heads = joined[:, :local_width].reshape(slab_len, head_count, HD)
    keys_here = joined[:, local_width : 2 * local_width]
    values_here = joined[:, 2 * local_width :]
    score_scale = HD ** (-0.5)
    blocks_here = key_slots.shape[0]
    slab_total = key_slots.shape[1]
    per_slab = key_slots.shape[2]
    block_rows = slab_len // blocks_here
    all_blocks = slab_total * per_slab
    block_ids = jnp.arange(per_slab, dtype=jnp.int32)
    listed = jnp.any(
        (key_slots[:, :, :, None] == block_ids[None, None, None, :])
        & (block_ids[None, None, :, None] < key_count[:, :, None, None]),
        axis=2,
    )
    allowed = listed.reshape(blocks_here, all_blocks).astype(jnp.float32)

    def compute(state, key_part, value_part, visible):
        row_count = key_part.shape[0]
        top_score, denominator, numerator = state
        scores = (
            jnp.einsum(
                "qhd,khd->hqk",
                query_heads,
                key_part.reshape(row_count, head_count, HD),
                preferred_element_type=jnp.float32,
            )
            * score_scale
        )
        scores = jnp.where(visible[None], scores, masked_score)
        new_top = jnp.maximum(top_score, jnp.max(scores, axis=-1))
        rescale = jnp.exp(top_score - new_top)
        shares = jnp.exp(scores - new_top[:, :, None])
        denominator = denominator * rescale + jnp.sum(shares, axis=-1)
        update = jnp.einsum(
            "hqk,khd->qhd",
            shares.astype(jnp.bfloat16),
            value_part.reshape(row_count, head_count, HD),
            preferred_element_type=jnp.float32,
        )
        numerator = numerator * jnp.transpose(rescale)[:, :, None] + update
        return (new_top, denominator, numerator)

    def attend_rows(running, key_part, value_part, first_row):
        row_count = key_part.shape[0]
        row_blocks = (first_row + jnp.arange(row_count, dtype=jnp.int32)) // block_rows
        onehot = (jnp.arange(all_blocks, dtype=jnp.int32)[:, None] == row_blocks[None, :]).astype(
            jnp.float32
        )
        listed_here = jnp.dot(allowed, onehot) > 0.5
        visible = jnp.broadcast_to(
            listed_here[:, None, :], (blocks_here, block_rows, row_count)
        ).reshape(slab_len, row_count)
        return compute(running, key_part, value_part, visible)

    initial = (
        jnp.full((head_count, slab_len), masked_score, jnp.float32),
        jnp.zeros((head_count, slab_len), jnp.float32),
        jnp.zeros((slab_len, head_count, HD), jnp.float32),
    )
    key_part = lax.all_gather(keys_here, "frame", axis=0, tiled=True)
    value_part = lax.all_gather(values_here, "frame", axis=0, tiled=True)
    row_count = key_part.shape[0]
    step_rows = 512

    def one_block(position, state):
        key_block = lax.dynamic_slice_in_dim(key_part, position * step_rows, step_rows, 0)
        value_block = lax.dynamic_slice_in_dim(value_part, position * step_rows, step_rows, 0)
        return attend_rows(state, key_block, value_block, position * step_rows)

    running = lax.fori_loop(0, row_count // step_rows, one_block, initial)
    top_score, denominator, numerator = running
    mixed = numerator / jnp.transpose(denominator)[:, :, None]
    return mixed.reshape(slab_len, local_width).astype(jnp.bfloat16)


def solution(mesh):
    return jax.shard_map(
        on_device,
        mesh=mesh,
        in_specs=(
            P(("video", "frame", "head"), None),
            P(None, None, "head"),
            P("frame", None, None),
            P("frame", None),
        ),
        out_specs=P(("video", "frame"), "head"),
        check_vma=False,
    )
```

profile of v0, /device:TPU:0, one launch (start us, length us, event | category | flops | bytes accessed | tf_op | source)
XLA Modules:
  0.0 130.2 jit_solution(18211134643761131619)
XLA Ops:
  6.5 0.7 all-gather.4.cloned.1.call-update
  7.3 13.8 %copy.22 = bf16[2560,3,640]{0,2,1:T(8,128)(2,1)} copy(bf16[2560,3,640]{2,0,1:T(8,128)(2,1)} %param.7) | data formatting | bytes 19660800 | tf_op args[1]
  21.1 8.7 %all-gather.4.cloned.1.call-done = bf16[256,2560]{1,0:T(8,128)(2,1)} async-done(((bf16[64,2560]{1,0:T(8,128)(2,1)}), bf16[256,2560]{1,0:T(8,128)(2,1)}) %all-gather.4.cloned.1.call-update) | async-done | bytes 1310736 | tf_op jit(solution)/shard_map/all_gather | solution.py:17
  29.8 7.1 %convolution_convert_fusion = bf16[256,1920]{1,0:T(8,128)(2,1)S(1)} fusion(bf16[256,2560]{1,0:T(8,128)(2,1)} %all-gather.4.cloned.1.call-done, bf16[2560,1920]{0,1:T(8,128)(2,1)} %bitcast.63), kind=kOutput, calls=%fused_computation.35 | convolution fusion | flops 2517073920 | bytes 12124160 | tf_op jit(solution)/shard_map/dot_general | solution.py:16
  37.0 0.9 fusion.26
  38.0 0.7 all-gather.8.cloned.1.call-update
  38.7 0.1 iota_compare_fusion.3
  38.8 0.1 fusion.25
  38.9 0.1 reshape.69
  39.0 0.2 copy.23
  39.2 0.9 copy.25
  40.1 30.7 %all-gather.6.cloned.1.call-done = bf16[1024,640]{1,0:T(8,128)(2,1)} async-done(((bf16[256,640]{1,0:T(8,128)(2,1)}), bf16[1024,640]{1,0:T(8,128)(2,1)}) %all-gather.6.cloned.1.call-update) | async-done | bytes 1310736 | tf_op jit(solution)/shard_map/all_gather | solution.py:83
  70.8 33.3 %all-gather.8.cloned.1.call-done = bf16[1024,640]{1,0:T(8,128)(2,1)} async-done(((bf16[256,640]{1,0:T(8,128)(2,1)}), bf16[1024,640]{1,0:T(8,128)(2,1)}) %all-gather.8.cloned.1.call-update) | async-done | bytes 1310736 | tf_op jit(solution)/shard_map/all_gather | solution.py:84
  104.1 17.6 %while.20 = (s32[]{:T(128)}, f32[5,256]{1,0:T(8,128)S(1)}, f32[5,256]{1,0:T(8,128)S(1)}, f32[256,5,128]{0,2,1:T(8,128)}, bf16[4,16]{1,0:T(4,128)(2,1)S(1)}, /*in...) while((s32[]{:T(128)}, f32[5,256]{1,0:T(8,128)S(1)}, ...), condition=%wide.region_4.5_spmd.clone, body=%wide.region_1.4_spmd.clone.sunk | while | flops 343336448 | bytes 16933176 | solution.py:93
  104.1 2.2 %constant_dynamic-slice_fusion.3 = (bf16[512,640]{1,0:T(8,128)(2,1)}, bf16[512,640]{1,0:T(8,128)(2,1)S(1)}) fusion(bf16[1024,640]{1,0:T(8,128)(2,1)} %get-tuple-element.375, s32[]{:T(128)S(6)} %select_n.63, bf16[1024,640]{1,0:T(8,128)(2,1)} %get-tuple-element.373), kind=kLoop, calls=%fused_computation.31.clone.1 | loop fusion | bytes 2621444 | tf_op jit(solution)/shard_map/while/body/eval_jaxpr/dynamic_slice | solution.py:90
  106.3 0.2 copy.36
  106.6 0.1 fusion.49
  106.8 0.3 copy.35
  107.0 1.6 %fusion.50 = (f32[5,256]{1,0:T(8,128)S(1)}, f32[5,512,256]{2,1,0:T(8,128)S(1)}) fusion(pred[256,512]{0,1:T(8,128)(4,1)S(1)} %copy.35, bf16[512,5,128]{0,2,1:T(8,128)(2,1)S(1)} %bitcast.60, bf16[256,5,128]{2,0,1:T(8,128)(2,1)} %get-tuple-element.374), kind=kOutput, calls=%fused_computation.4.clone.1 | convolution fusion | flops 169736960 | bytes 3740672 | tf_op jit(solution)/shard_map/while/body/eval_jaxpr/qhd,khd->hqk/dot_general | solution.py:44
  108.7 1.3 %copy.37 = bf16[512,640]{0,1:T(8,128)(2,1)S(1)} copy(bf16[512,640]{1,0:T(8,128)(2,1)} %get-tuple-element.342) | data formatting | bytes 1310720 | tf_op jit(solution)/shard_map/while/body/eval_jaxpr/dynamic_slice | solution.py:90
  110.0 1.7 %fusion.54 = f32[256,5,128]{0,2,1:T(8,128)} fusion(bf16[512,5,128]{0,2,1:T(8,128)(2,1)S(1)} %bitcast.61, f32[5,512,256]{2,1,0:T(8,128)S(1)} %get-tuple-element.341, f32[5,256]{1,0:T(8,128)S(1)} %get-tuple-element.369, pred[256,512]{0,1:T(8,128)(4,1)S(1)} %copy.35, f32[256,5,128]{0,2,1:T(8,128)} %get-tuple-element.359, ...), kind=kOutput, calls=%fused_computation.11.clone.1 | convolution fusion | flops 170885120 | bytes 4728833 | tf_op jit(solution)/shard_map/while/body/eval_jaxpr/hqk,khd->qhd/dot_general | solution.py:57
  111.7 0.6 fusion.52
  112.3 2.2 %constant_dynamic-slice_fusion.3 = (bf16[512,640]{1,0:T(8,128)(2,1)}, bf16[512,640]{1,0:T(8,128)(2,1)S(1)}) fusion(bf16[1024,640]{1,0:T(8,128)(2,1)} %get-tuple-element.375, s32[]{:T(128)S(6)} %select_n.63, bf16[1024,640]{1,0:T(8,128)(2,1)} %get-tuple-element.373), kind=kLoop, calls=%fused_computation.31.clone.1 | loop fusion | bytes 2621444 | tf_op jit(solution)/shard_map/while/body/eval_jaxpr/dynamic_slice | solution.py:90
  114.6 0.2 copy.36
  114.8 0.1 fusion.49
  115.0 0.3 copy.35
  115.3 1.6 %fusion.50 = (f32[5,256]{1,0:T(8,128)S(1)}, f32[5,512,256]{2,1,0:T(8,128)S(1)}) fusion(pred[256,512]{0,1:T(8,128)(4,1)S(1)} %copy.35, bf16[512,5,128]{0,2,1:T(8,128)(2,1)S(1)} %bitcast.60, bf16[256,5,128]{2,0,1:T(8,128)(2,1)} %get-tuple-element.374), kind=kOutput, calls=%fused_computation.4.clone.1 | convolution fusion | flops 169736960 | bytes 3740672 | tf_op jit(solution)/shard_map/while/body/eval_jaxpr/qhd,khd->hqk/dot_general | solution.py:44
  116.9 1.3 %copy.37 = bf16[512,640]{0,1:T(8,128)(2,1)S(1)} copy(bf16[512,640]{1,0:T(8,128)(2,1)} %get-tuple-element.342) | data formatting | bytes 1310720 | tf_op jit(solution)/shard_map/while/body/eval_jaxpr/dynamic_slice | solution.py:90
  118.3 2.8 %fusion.54 = f32[256,5,128]{0,2,1:T(8,128)} fusion(bf16[512,5,128]{0,2,1:T(8,128)(2,1)S(1)} %bitcast.61, f32[5,512,256]{2,1,0:T(8,128)S(1)} %get-tuple-element.341, f32[5,256]{1,0:T(8,128)S(1)} %get-tuple-element.369, pred[256,512]{0,1:T(8,128)(4,1)S(1)} %copy.35, f32[256,5,128]{0,2,1:T(8,128)} %get-tuple-element.359, ...), kind=kOutput, calls=%fused_computation.11.clone.1 | convolution fusion | flops 170885120 | bytes 4728833 | tf_op jit(solution)/shard_map/while/body/eval_jaxpr/hqk,khd->qhd/dot_general | solution.py:57
  121.0 0.6 fusion.52
  121.6 1.1 divide_convert_fusion
  122.8 0.9 copy.27
  (22 shorter events, 0.3 us)
Async XLA Ops:
  6.5 23.3 %all-gather.4.cloned.1.call-start = ((), (), s32[]{:S(2)}) async-start(), calls=%async_computation | async-start | bytes 1638400 | tf_op jit(solution)/shard_map/all_gather | solution.py:17
  7.3 63.5 %all-gather.6.cloned.1.call-start = ((), (), s32[]{:S(2)}) async-start(), calls=%async_computation.1 | async-start | bytes 1638400 | tf_op jit(solution)/shard_map/all_gather | solution.py:83
  36.9 1.7 %copy-start.1 = (s32[4,4]{1,0:T(4,128)S(1)}, s32[4,4]{1,0:T(4,128)}, u32[]{:S(2)}) copy-start(s32[4,4]{1,0:T(4,128)} %param.9) | copy-start | bytes 196
  37.0 1.8 %copy-start = (s32[4,4,4]{2,1,0:T(4,128)S(1)}, s32[4,4,4]{2,1,0:T(4,128)}, u32[]{:S(2)}) copy-start(s32[4,4,4]{2,1,0:T(4,128)} %param.8) | copy-start | bytes 772
  37.9 66.2 %all-gather.8.cloned.1.call-start = ((), (), s32[]{:S(2)}) async-start(), calls=%async_computation.2 | async-start | bytes 1638400 | tf_op jit(solution)/shard_map/all_gather | solution.py:84
Sparse Core Ops, SparseCore 0:
  8.9 20.8 all-gather.3
  38.0 32.6 all-gather.5
  72.3 31.6 all-gather.7
where the time goes:
time: 131 us; the launch traced here: 130 us
  waiting for transfers between devices  74.1 us (57%)
  local copies, waits for them, and re-layouts  25.1 us (19%)
  matrix products  15.1 us (12%)
  between operations  13.2 us (10%)
  other arithmetic  2.52 us (2%)
    all_gather x1, waiting for transfers between devices, on_device(): value_part = lax.all_gather(values_here, 'frame', axis=0, tiled=True)  33.3 us
    all_gather x1, waiting for transfers between devices, on_device(): key_part = lax.all_gather(keys_here, 'frame', axis=0, tiled=True)  30.7 us
    unnamed x6, local copies, waits for them, and re-layouts  14.7 us
    all_gather x1, waiting for transfers between devices, on_device(): lax.all_gather(latents, 'head', axis=0, tiled=True)  8.7 us
    dynamic_slice x4, local copies, waits for them, and re-layouts, one_block(): lax.dynamic_slice_in_dim(value_part, position * step_rows, step_rows, 0)  7.14 us
    dot_general x1, matrix products, on_device(): jnp.dot(lax.all_gather(latents, 'head', axis=0, tiled=True), w_joined, pr...  7.09 us
    dot_general x2, matrix products, compute(): jnp.einsum('hqk,khd->qhd', shares.astype(jnp.bfloat16), value_part.reshap...  4.46 us
    dot_general x2, matrix products, compute(): jnp.einsum('qhd,khd->hqk', query_heads, key_part.reshape(row_count, head_...  3.27 us
  transfers between devices with their start and end apart: 3, of which 3 were waited for; matrix products, arithmetic and copies ran while one was open for 12% of the time, Pallas kernels for 0%

commit v1 on v0

--- a/solution.py
+++ b/solution.py
@@ -1,12 +1,17 @@
+import functools
+
 import jax
 import jax.numpy as jnp
 from jax import lax
+from jax.experimental import pallas as pl
+from jax.experimental.pallas import tpu as pltpu
 from jax.sharding import PartitionSpec as P
 
 HD = 128
 
 
 masked_score = -1e30
+MESH = pl.DeviceIdType.MESH
 
 
 def on_device(latents, weights, key_slots, key_count):
@@ -96,9 +101,224 @@
     return mixed.reshape(slab_len, local_width).astype(jnp.bfloat16)
 
 
+def kernel(lat, w_hbm, slots, count, out, tokens, w, w_sem, kv, q, top, total, acc, send_sem, recv_sem):
+    z = lax.axis_index("frame")
+    h = lax.axis_index("head")
+    core = h % 2
+    mate = h + 1 - 2 * core
+    across = (h + 2) % 4
+    rows, width_in = lat.shape
+    width = w_hbm.shape[2]
+    slab = 4 * rows
+    heads = width // HD
+    blocks = slots.shape[0]
+    per_slab = slots.shape[2]
+    block_rows = slab // blocks
+    key_rows = slab // per_slab
+    scale = HD ** (-0.5)
+
+    w_copies = [
+        pltpu.make_async_copy(w_hbm.at[j], w.at[:, pl.ds(place * width, width)], w_sem.at[place])
+        for place, j in enumerate((1, 2, 0))
+    ]
+    for copy in w_copies:
+        copy.start()
+
+    half = z // 2
+    end = z + half * (3 - 2 * z)
+    firsts = [1 - end, 2, 3]
+    others = [f + half * (3 - 2 * f) for f in firsts]
+
+    barrier = pltpu.get_barrier_semaphore()
+
+    def greet(frame, who):
+        pl.semaphore_signal(barrier, inc=1, device_id={"frame": frame, "head": who}, device_id_type=MESH)
+
+    greet(z, mate)
+    greet(z, across)
+
+    @pl.when(z > 0)
+    def _():
+        greet(z - 1, h)
+
+    @pl.when(z < 3)
+    def _():
+        greet(z + 1, h)
+
+    pl.semaphore_wait(barrier, jnp.where(end == 0, 3, 4))
+
+    def copy_of(src, slot, number, frame, who):
+        return pltpu.make_async_remote_copy(
+            src_ref=src,
+            dst_ref=tokens.at[slot],
+            send_sem=send_sem.at[number],
+            recv_sem=recv_sem.at[slot],
+            device_id={"frame": frame, "head": who},
+            device_id_type=MESH,
+        )
+
+    sends = []
+
+    def send(src, slot, frame, who, when=None):
+        copy = copy_of(src, slot, len(sends), frame, who)
+        sends.append((copy, when))
+        if when is None:
+            copy.start()
+        else:
+            pl.when(when)(copy.start)
+
+    def arrived(slot):
+        copy_of(tokens.at[slot], slot, 0, z, mate).wait_recv()
+
+    mine = z * 4 + h
+    send(lat, mine, z, across)
+    send(lat, mine, z - 1, h, z > 0)
+    send(lat, mine, z + 1, h, z < 3)
+    send(lat, mine, z, mate)
+    tokens[mine] = lat[...]
+
+    def forward(number, when):
+        b = others[number]
+        slot = b * 4 + h
+        sign = jnp.where(b > z, 1, -1)
+        onward = z - sign
+        goes = (onward >= 0) & (onward <= 3)
+        base = 4 + 3 * number
+        moves = [
+            (copy_of(tokens.at[slot], slot, base, onward, h), goes),
+            (copy_of(tokens.at[slot], slot, base + 1, z, across), None),
+            (copy_of(tokens.at[slot], slot, base + 2, z, mate), None),
+        ]
+
+        def go():
+            arrived(slot)
+            pl.when(goes)(moves[0][0].start)
+            moves[1][0].start()
+            moves[2][0].start()
+
+        if when is None:
+            go()
+        else:
+            pl.when(when)(go)
+        return moves
+
+    def complete(number, b):
+        slot = b * 4 + across
+        arrived(slot)
+        copy = copy_of(tokens.at[slot], slot, 13 + number, z, mate)
+        copy.start()
+        arrived(b * 4 + mate)
+        arrived(b * 4 + (mate + 2) % 4)
+        return [(copy, None)]
+
+    def project(b, first, columns, store):
+        x = tokens[pl.ds(b * 4, 4)].reshape(slab, width_in)
+        part = jnp.dot(x, w[:, pl.ds(first, columns)], preferred_element_type=jnp.float32)
+        store[...] = part.astype(jnp.bfloat16)
+
+    def attend(b, first):
+        for tile in range(2 * width // 256):
+            project(b, tile * 256, 256, kv.at[:, pl.ds(tile * 256, 256)])
+        lane_block = lax.broadcasted_iota(jnp.int32, (1, slab), 1) // key_rows
+        shades = []
+        for a in range(blocks):
+            listed = count[a, b]
+            seen = jnp.zeros((1, slab), jnp.float32)
+            for s in range(per_slab):
+                wanted = jnp.where(s < listed, slots[a, b, s], -1)
+                seen = jnp.where(lane_block == wanted, 1.0, seen)
+            shade = jnp.where(seen > 0.5, 0.0, masked_score)
+            shades.append(jnp.broadcast_to(shade, (block_rows, slab)))
+        shade = jnp.concatenate(shades, axis=0)
+        for n in range(heads):
+            cols = pl.ds(n * HD, HD)
+            scores = lax.dot_general(
+                q[:, cols], kv[:, cols], (((1,), (1,)), ((), ())), preferred_element_type=jnp.float32
+            )
+            scores = scores * scale + shade
+            peak = jnp.max(scores, axis=1, keepdims=True)
+            if not first:
+                peak = jnp.maximum(peak, top[n])
+            shares = jnp.exp(scores - peak)
+            added = jnp.sum(shares, axis=1, keepdims=True)
+            mixed = jnp.dot(
+                shares.astype(jnp.bfloat16),
+                kv[:, pl.ds(width + n * HD, HD)],
+                preferred_element_type=jnp.float32,
+            )
+            if not first:
+                keep = jnp.exp(top[n] - peak)
+                added = added + total[n] * keep
+                mixed = mixed + acc[n] * keep
+            top[n] = peak
+            total[n] = added
+            acc[n] = mixed
+
+    middle = end == 1
+    outer = end == 0
+    late = []
+    late += forward(0, None)
+    late += forward(1, middle)
+    late += complete(0, z)
+    for copy in w_copies:
+        copy.wait()
+    project(z, 2 * width, width, q)
+    attend(z, True)
+    forward(1, outer)
+    late += forward(2, middle)
+    late += complete(1, others[0])
+    attend(others[0], False)
+    forward(2, outer)
+    late += complete(2, others[1])
+    attend(others[1], False)
+    late += complete(3, others[2])
+    attend(others[2], False)
+    for n in range(heads):
+        out[:, pl.ds(n * HD, HD)] = (acc[n] / total[n]).astype(jnp.bfloat16)
+    for copy, when in sends + late:
+        if when is None:
+            copy.wait_send()
+        else:
+            pl.when(when)(copy.wait_send)
+
+
+def fused(latents, weights, key_slots, key_count):
+    rows, width_in = latents.shape
+    width = weights.shape[2]
+    slab = 4 * rows
+    heads = width // HD
+    return pl.pallas_call(
+        kernel,
+        out_shape=jax.ShapeDtypeStruct((slab, width), jnp.bfloat16),
+        in_specs=[
+            pl.BlockSpec(memory_space=pltpu.VMEM),
+            pl.BlockSpec(memory_space=pl.ANY),
+            pl.BlockSpec(memory_space=pltpu.SMEM),
+            pl.BlockSpec(memory_space=pltpu.SMEM),
+        ],
+        out_specs=pl.BlockSpec(memory_space=pltpu.VMEM),
+        scratch_shapes=[
+            pltpu.VMEM((16, rows, width_in), jnp.bfloat16),
+            pltpu.VMEM((width_in, 3 * width), jnp.bfloat16),
+            pltpu.SemaphoreType.DMA((3,)),
+            pltpu.VMEM((slab, 2 * width), jnp.bfloat16),
+            pltpu.VMEM((slab, width), jnp.bfloat16),
+            pltpu.VMEM((heads, slab, 1), jnp.float32),
+            pltpu.VMEM((heads, slab, 1), jnp.float32),
+            pltpu.VMEM((heads, slab, HD), jnp.float32),
+            pltpu.SemaphoreType.DMA((17,)),
+            pltpu.SemaphoreType.DMA((16,)),
+        ],
+        compiler_params=pltpu.CompilerParams(
+            collective_id=0, has_side_effects=True, vmem_limit_bytes=48 * 1024 * 1024
+        ),
+    )(latents, jnp.transpose(weights, (1, 0, 2)), key_slots, key_count)
+
+
 def solution(mesh):
+    small = mesh.shape["frame"] == 4 and mesh.shape["head"] == 4
     return jax.shard_map(
-        on_device,
+        fused if small else on_device,
         mesh=mesh,
         in_specs=(
             P(("video", "frame", "head"), None),

time: 131 us -> 45.1 us (0.34)
  the two profiles are of different devices: /device:TPU:0 before, /device:TPU:1 now
where the time goes in v1:
time: 45.1 us; the launch traced here: 44.9 us
  Pallas kernels  41.8 us (93%)
  local copies, waits for them, and re-layouts  3.08 us (7%)
    pallas_call x1, Pallas kernels, fused(): pl.pallas_call(kernel, out_shape=jax.ShapeDtypeStruct((slab, width), jnp....  41.8 us
    unnamed x7, local copies, waits for them, and re-layouts  3.08 us

profile of v1, /device:TPU:1, one launch (start us, length us, event | category | flops | bytes accessed | tf_op | source)
XLA Modules:
  0.0 44.9 jit_solution(5949807218234818679)
XLA Ops:
  0.0 0.0 copy-start
  0.0 1.0 %copy-done = bf16[64,2560]{1,0:T(8,128)(2,1)S(1)} copy-done((bf16[64,2560]{1,0:T(8,128)(2,1)S(1)}, bf16[64,2560]{1,0:T(8,128)(2,1)}, u32[]{:S(2)}) %copy-start) | copy-done | bytes 327704
  1.0 0.0 copy-start.1
  1.0 0.7 %copy-done.1 = s32[4,4,4]{2,1,0:T(4,128)S(1)} copy-done((s32[4,4,4]{2,1,0:T(4,128)S(1)}, s32[4,4,4]{2,1,0:T(4,128)}, u32[]{:S(2)}) %copy-start.1) | copy-done | bytes 280
  1.7 0.0 copy-start.2
  1.7 0.7 %copy-done.2 = s32[4,4]{1,0:T(4,128)S(1)} copy-done((s32[4,4]{1,0:T(4,128)S(1)}, s32[4,4]{1,0:T(4,128)}, u32[]{:S(2)}) %copy-start.2) | copy-done | bytes 88
  2.4 41.8 %shard_map.46 = bf16[256,640]{1,0:T(8,128)(2,1)S(1)} custom-call(bf16[64,2560]{1,0:T(8,128)(2,1)S(1)} %copy-done, bf16[3,2560,640]{2,1,0:T(8,128)(2,1)} %bitcast.1, s32[4,4,4]{2,1,0:T(4,128)S(1)} %copy-done.1, s32[4,4]{1,0:T(4,128)S(1)} %copy-done.2), custom_call_target="tpu_custom_call" | custom-call | tf_op jit(solution)/shard_map/pallas_call | solution.py:290
  44.1 0.7 %copy.6 = bf16[256,640]{1,0:T(8,128)(2,1)} copy(bf16[256,640]{1,0:T(8,128)(2,1)S(1)} %shard_map.46) | data formatting | bytes 655360
Async XLA Ops:
  0.0 1.0 %copy-start = (bf16[64,2560]{1,0:T(8,128)(2,1)S(1)}, bf16[64,2560]{1,0:T(8,128)(2,1)}, u32[]{:S(2)}) copy-start(bf16[64,2560]{1,0:T(8,128)(2,1)} %lat.1) | copy-start | bytes 983044
  1.0 0.7 %copy-start.1 = (s32[4,4,4]{2,1,0:T(4,128)S(1)}, s32[4,4,4]{2,1,0:T(4,128)}, u32[]{:S(2)}) copy-start(s32[4,4,4]{2,1,0:T(4,128)} %slots.1) | copy-start | bytes 772
  1.7 0.7 %copy-start.2 = (s32[4,4]{1,0:T(4,128)S(1)}, s32[4,4]{1,0:T(4,128)}, u32[]{:S(2)}) copy-start(s32[4,4]{1,0:T(4,128)} %count.1) | copy-start | bytes 196

commit v2 on v1

--- a/solution.py
+++ b/solution.py
@@ -101,7 +101,7 @@
     return mixed.reshape(slab_len, local_width).astype(jnp.bfloat16)
 
 
-def kernel(lat, w_hbm, slots, count, out, tokens, w, w_sem, kv, q, top, total, acc, send_sem, recv_sem):
+def kernel(lat, w_hbm, slots_hbm, count_hbm, out, slots, count, local_sem, tokens, w, w_sem, kv, q, top, total, acc, send_sem, recv_sem):
     z = lax.axis_index("frame")
     h = lax.axis_index("head")
     core = h % 2
@@ -175,7 +175,13 @@
     send(lat, mine, z - 1, h, z > 0)
     send(lat, mine, z + 1, h, z < 3)
     send(lat, mine, z, mate)
-    tokens[mine] = lat[...]
+    local = [
+        pltpu.make_async_copy(lat, tokens.at[mine], local_sem.at[0]),
+        pltpu.make_async_copy(slots_hbm, slots, local_sem.at[1]),
+        pltpu.make_async_copy(count_hbm, count, local_sem.at[2]),
+    ]
+    for copy in local:
+        copy.start()
 
     def forward(number, when):
         b = others[number]
@@ -207,33 +213,33 @@
         arrived(slot)
         copy = copy_of(tokens.at[slot], slot, 13 + number, z, mate)
         copy.start()
-        arrived(b * 4 + mate)
         arrived(b * 4 + (mate + 2) % 4)
         return [(copy, None)]
 
-    def project(b, first, columns, store):
-        x = tokens[pl.ds(b * 4, 4)].reshape(slab, width_in)
+    def project(slot, rows_here, first, columns, store):
+        x = tokens[pl.ds(slot, rows_here // rows)].reshape(rows_here, width_in)
         part = jnp.dot(x, w[:, pl.ds(first, columns)], preferred_element_type=jnp.float32)
         store[...] = part.astype(jnp.bfloat16)
 
-    def attend(b, first):
+    def attend(b, place, length, first):
+        span = length * rows
         for tile in range(2 * width // 256):
-            project(b, tile * 256, 256, kv.at[:, pl.ds(tile * 256, 256)])
-        lane_block = lax.broadcasted_iota(jnp.int32, (1, slab), 1) // key_rows
+            project(b * 4 + place, span, tile * 256, 256, kv.at[pl.ds(0, span), pl.ds(tile * 256, 256)])
+        lane_block = (lax.broadcasted_iota(jnp.int32, (1, span), 1) + place * rows) // key_rows
         shades = []
         for a in range(blocks):
             listed = count[a, b]
-            seen = jnp.zeros((1, slab), jnp.float32)
+            seen = jnp.zeros((1, span), jnp.float32)
             for s in range(per_slab):
                 wanted = jnp.where(s < listed, slots[a, b, s], -1)
                 seen = jnp.where(lane_block == wanted, 1.0, seen)
             shade = jnp.where(seen > 0.5, 0.0, masked_score)
-            shades.append(jnp.broadcast_to(shade, (block_rows, slab)))
+            shades.append(jnp.broadcast_to(shade, (block_rows, span)))
         shade = jnp.concatenate(shades, axis=0)
         for n in range(heads):
             cols = pl.ds(n * HD, HD)
             scores = lax.dot_general(
-                q[:, cols], kv[:, cols], (((1,), (1,)), ((), ())), preferred_element_type=jnp.float32
+                q[:, cols], kv[pl.ds(0, span), cols], (((1,), (1,)), ((), ())), preferred_element_type=jnp.float32
             )
             scores = scores * scale + shade
             peak = jnp.max(scores, axis=1, keepdims=True)
@@ -243,7 +249,7 @@
             added = jnp.sum(shares, axis=1, keepdims=True)
             mixed = jnp.dot(
                 shares.astype(jnp.bfloat16),
-                kv[:, pl.ds(width + n * HD, HD)],
+                kv[pl.ds(0, span), pl.ds(width + n * HD, HD)],
                 preferred_element_type=jnp.float32,
             )
             if not first:
@@ -260,19 +266,25 @@
     late += forward(0, None)
     late += forward(1, middle)
     late += complete(0, z)
-    for copy in w_copies:
+    arrived(z * 4 + mate)
+    for copy in local + w_copies:
         copy.wait()
-    project(z, 2 * width, width, q)
-    attend(z, True)
+    project(z * 4, slab, 2 * width, width, q)
+    attend(z, 0, 4, True)
     forward(1, outer)
     late += forward(2, middle)
     late += complete(1, others[0])
-    attend(others[0], False)
+    arrived(others[0] * 4 + mate)
+    attend(others[0], 0, 4, False)
     forward(2, outer)
     late += complete(2, others[1])
-    attend(others[1], False)
+    arrived(others[1] * 4 + mate)
+    attend(others[1], 0, 4, False)
+    near = 2 * (h // 2)
+    arrived(others[2] * 4 + mate)
+    attend(others[2], near, 2, False)
     late += complete(3, others[2])
-    attend(others[2], False)
+    attend(others[2], 2 - near, 2, False)
     for n in range(heads):
         out[:, pl.ds(n * HD, HD)] = (acc[n] / total[n]).astype(jnp.bfloat16)
     for copy, when in sends + late:
@@ -291,13 +303,16 @@
         kernel,
         out_shape=jax.ShapeDtypeStruct((slab, width), jnp.bfloat16),
         in_specs=[
-            pl.BlockSpec(memory_space=pltpu.VMEM),
-            pl.BlockSpec(memory_space=pl.ANY),
-            pl.BlockSpec(memory_space=pltpu.SMEM),
-            pl.BlockSpec(memory_space=pltpu.SMEM),
+            pl.BlockSpec(memory_space=pltpu.HBM),
+            pl.BlockSpec(memory_space=pltpu.HBM),
+            pl.BlockSpec(memory_space=pltpu.HBM),
+            pl.BlockSpec(memory_space=pltpu.HBM),
         ],
         out_specs=pl.BlockSpec(memory_space=pltpu.VMEM),
         scratch_shapes=[
+            pltpu.SMEM(key_slots.shape, jnp.int32),
+            pltpu.SMEM(key_count.shape, jnp.int32),
+            pltpu.SemaphoreType.DMA((3,)),
             pltpu.VMEM((16, rows, width_in), jnp.bfloat16),
             pltpu.VMEM((width_in, 3 * width), jnp.bfloat16),
             pltpu.SemaphoreType.DMA((3,)),
@@ -310,7 +325,7 @@
             pltpu.SemaphoreType.DMA((16,)),
         ],
         compiler_params=pltpu.CompilerParams(
-            collective_id=0, has_side_effects=True, vmem_limit_bytes=48 * 1024 * 1024
+            collective_id=0, has_side_effects=True, vmem_limit_bytes=64 * 1024 * 1024
         ),
     )(latents, jnp.transpose(weights, (1, 0, 2)), key_slots, key_count)
 

time: 45.1 us -> 43.2 us (0.958)
  the two profiles are of different devices: /device:TPU:1 before, /device:TPU:0 now
where the time goes in v2:
time: 43.2 us; the launch traced here: 42.8 us
  Pallas kernels  41.1 us (95%)
  local copies, waits for them, and re-layouts  1.73 us (4%)
    pallas_call x1, Pallas kernels, fused(): pl.pallas_call(kernel, out_shape=jax.ShapeDtypeStruct((slab, width), jnp....  41.1 us
    unnamed x1, local copies, waits for them, and re-layouts  1.73 us

profile of v2, /device:TPU:0, one launch (start us, length us, event | category | flops | bytes accessed | tf_op | source)
XLA Modules:
  0.0 42.8 jit_solution(11388814897694912317)
XLA Ops:
  0.0 41.1 %shard_map.46 = bf16[256,640]{1,0:T(8,128)(2,1)} custom-call(bf16[64,2560]{1,0:T(8,128)(2,1)} %lat.1, bf16[3,2560,640]{2,1,0:T(8,128)(2,1)} %bitcast.1, s32[4,4,4]{2,1,0:T(4,128)} %slots_hbm.1, s32[4,4]{1,0:T(4,128)} %count_hbm.1), custom_call_target="tpu_custom_call" | custom-call | tf_op jit(solution)/shard_map/pallas_call | solution.py:302
  41.1 1.7 %copy.6 = bf16[256,640]{1,0:T(8,128)(2,1)} copy(bf16[256,640]{1,0:T(8,128)(2,1)} %shard_map.46) | data formatting | bytes 655360

commit v3 on v2

--- a/solution.py
+++ b/solution.py
@@ -101,7 +101,7 @@
     return mixed.reshape(slab_len, local_width).astype(jnp.bfloat16)
 
 
-def kernel(lat, w_hbm, slots_hbm, count_hbm, out, slots, count, local_sem, tokens, w, w_sem, kv, q, top, total, acc, send_sem, recv_sem):
+def kernel(lat, w_hbm, slots_hbm, count_hbm, out, slots, count, local_sem, tokens, w, w_sem, kv, q, top, total, acc, send_sem, recv_sem, up_sem):
     z = lax.axis_index("frame")
     h = lax.axis_index("head")
     core = h % 2
@@ -157,6 +157,30 @@
             device_id_type=MESH,
         )
 
+    def lower_of(slot, number, frame, who):
+        part = tokens.at[slot, pl.ds(0, rows // 2)]
+        return pltpu.make_async_remote_copy(
+            src_ref=part,
+            dst_ref=part,
+            send_sem=send_sem.at[number],
+            recv_sem=recv_sem.at[slot],
+            device_id={"frame": frame, "head": who},
+            device_id_type=MESH,
+        )
+
+    def upper_of(b, number, frame):
+        part = tokens.at[b * 4 + across, pl.ds(rows // 2, rows // 2)]
+        return pltpu.make_async_remote_copy(
+            src_ref=part,
+            dst_ref=tokens.at[b * 4 + across, pl.ds(rows // 2, rows // 2)],
+            send_sem=send_sem.at[number],
+            recv_sem=up_sem.at[b // 3],
+            device_id={"frame": frame, "head": h},
+            device_id_type=MESH,
+        )
+
+    middle = end == 1
+    outer = end == 0
     sends = []
 
     def send(src, slot, frame, who, when=None):
@@ -192,15 +216,23 @@
         base = 4 + 3 * number
         moves = [
             (copy_of(tokens.at[slot], slot, base, onward, h), goes),
-            (copy_of(tokens.at[slot], slot, base + 1, z, across), None),
             (copy_of(tokens.at[slot], slot, base + 2, z, mate), None),
         ]
+        if number == 0:
+            moves.append((copy_of(tokens.at[slot], slot, base + 1, z, across), outer))
+            moves.append((lower_of(slot, base + 1, z, across), middle))
+        elif number == 1:
+            moves.append((copy_of(tokens.at[slot], slot, base + 1, z, across), None))
+        else:
+            moves.append((lower_of(slot, base + 1, z, across), None))
 
         def go():
             arrived(slot)
-            pl.when(goes)(moves[0][0].start)
-            moves[1][0].start()
-            moves[2][0].start()
+            for copy, wanted in moves[:1] + moves[2:] + moves[1:2]:
+                if wanted is None:
+                    copy.start()
+                else:
+                    pl.when(wanted)(copy.start)
 
         if when is None:
             go()
@@ -210,11 +242,41 @@
 
     def complete(number, b):
         slot = b * 4 + across
-        arrived(slot)
+        if number == 1:
+
+            @pl.when(outer)
+            def _():
+                arrived(slot)
+
+            @pl.when(middle)
+            def _():
+                lower_of(slot, 0, z, mate).wait_recv()
+
+        elif number == 3:
+            lower_of(slot, 0, z, mate).wait_recv()
+
+            @pl.when(outer)
+            def _():
+                upper_of(b, 0, z + 1 - 2 * half).wait_recv()
+
+        else:
+            arrived(slot)
         copy = copy_of(tokens.at[slot], slot, 13 + number, z, mate)
         copy.start()
         arrived(b * 4 + (mate + 2) % 4)
         return [(copy, None)]
+
+    inward = z + 1 - 2 * half
+
+    def pass_upper(b, number, frame):
+        copy = upper_of(b, number, frame)
+
+        @pl.when(middle)
+        def _():
+            copy.wait_recv()
+            copy.start()
+
+        return [(copy, middle)]
 
     def project(slot, rows_here, first, columns, store):
         x = tokens[pl.ds(slot, rows_here // rows)].reshape(rows_here, width_in)
@@ -260,12 +322,13 @@
             total[n] = added
             acc[n] = mixed
 
-    middle = end == 1
-    outer = end == 0
     late = []
     late += forward(0, None)
     late += forward(1, middle)
     late += complete(0, z)
+    own_upper = upper_of(z, 17, inward)
+    pl.when(outer)(own_upper.start)
+    late.append((own_upper, outer))
     arrived(z * 4 + mate)
     for copy in local + w_copies:
         copy.wait()
@@ -273,10 +336,12 @@
     attend(z, 0, 4, True)
     forward(1, outer)
     late += forward(2, middle)
+    late += pass_upper(others[0], 18, inward)
     late += complete(1, others[0])
     arrived(others[0] * 4 + mate)
     attend(others[0], 0, 4, False)
     forward(2, outer)
+    late += pass_upper(others[2], 19, z - 1 + 2 * half)
     late += complete(2, others[1])
     arrived(others[1] * 4 + mate)
     attend(others[1], 0, 4, False)
@@ -321,8 +386,9 @@
             pltpu.VMEM((heads, slab, 1), jnp.float32),
             pltpu.VMEM((heads, slab, 1), jnp.float32),
             pltpu.VMEM((heads, slab, HD), jnp.float32),
-            pltpu.SemaphoreType.DMA((17,)),
+            pltpu.SemaphoreType.DMA((20,)),
             pltpu.SemaphoreType.DMA((16,)),
+            pltpu.SemaphoreType.DMA((2,)),
         ],
         compiler_params=pltpu.CompilerParams(
             collective_id=0, has_side_effects=True, vmem_limit_bytes=64 * 1024 * 1024

time: 43.2 us -> 43 us (level)
  no operation moved by 1% of the time
where the time goes in v3:
time: 43 us; the launch traced here: 42.9 us
  Pallas kernels  41.1 us (96%)
  local copies, waits for them, and re-layouts  1.73 us (4%)
    pallas_call x1, Pallas kernels, fused(): pl.pallas_call(kernel, out_shape=jax.ShapeDtypeStruct((slab, width), jnp....  41.1 us
    unnamed x1, local copies, waits for them, and re-layouts  1.73 us

profile of v3, /device:TPU:0, one launch (start us, length us, event | category | flops | bytes accessed | tf_op | source)
XLA Modules:
  0.0 42.9 jit_solution(6309983494664570310)
XLA Ops:
  0.0 41.1 %shard_map.46 = bf16[256,640]{1,0:T(8,128)(2,1)} custom-call(bf16[64,2560]{1,0:T(8,128)(2,1)} %lat.1, bf16[3,2560,640]{2,1,0:T(8,128)(2,1)} %bitcast.1, s32[4,4,4]{2,1,0:T(4,128)} %slots_hbm.1, s32[4,4]{1,0:T(4,128)} %count_hbm.1), custom_call_target="tpu_custom_call" | custom-call | tf_op jit(solution)/shard_map/pallas_call | solution.py:367
  41.1 1.7 %copy.6 = bf16[256,640]{1,0:T(8,128)(2,1)} copy(bf16[256,640]{1,0:T(8,128)(2,1)} %shard_map.46) | data formatting | bytes 655360

commit v4 on v3

--- a/solution.py
+++ b/solution.py
@@ -115,7 +115,7 @@
     per_slab = slots.shape[2]
     block_rows = slab // blocks
     key_rows = slab // per_slab
-    scale = HD ** (-0.5)
+    scale = HD ** (-0.5) * 1.4426950408889634
 
     w_copies = [
         pltpu.make_async_copy(w_hbm.at[j], w.at[:, pl.ds(place * width, width)], w_sem.at[place])
@@ -307,7 +307,7 @@
             peak = jnp.max(scores, axis=1, keepdims=True)
             if not first:
                 peak = jnp.maximum(peak, top[n])
-            shares = jnp.exp(scores - peak)
+            shares = jnp.exp2(scores - peak)
             added = jnp.sum(shares, axis=1, keepdims=True)
             mixed = jnp.dot(
                 shares.astype(jnp.bfloat16),
@@ -315,7 +315,7 @@
                 preferred_element_type=jnp.float32,
             )
             if not first:
-                keep = jnp.exp(top[n] - peak)
+                keep = jnp.exp2(top[n] - peak)
                 added = added + total[n] * keep
                 mixed = mixed + acc[n] * keep
             top[n] = peak
@@ -345,11 +345,9 @@
     late += complete(2, others[1])
     arrived(others[1] * 4 + mate)
     attend(others[1], 0, 4, False)
-    near = 2 * (h // 2)
     arrived(others[2] * 4 + mate)
-    attend(others[2], near, 2, False)
     late += complete(3, others[2])
-    attend(others[2], 2 - near, 2, False)
+    attend(others[2], 0, 4, False)
     for n in range(heads):
         out[:, pl.ds(n * HD, HD)] = (acc[n] / total[n]).astype(jnp.bfloat16)
     for copy, when in sends + late:

time: 43 us -> 41.4 us (0.963)
  Pallas kernels: 41.1 us -> 39.5 us
    pallas_call x1, Pallas kernels: 41.1 us -> 39.5 us  [fused(): pl.pallas_call(kernel, out_shape=jax.ShapeDtypeStruct((slab, width), jnp....]
where the time goes in v4:
time: 41.4 us; the launch traced here: 41.2 us
  Pallas kernels  39.5 us (95%)
  local copies, waits for them, and re-layouts  1.73 us (4%)
    pallas_call x1, Pallas kernels, fused(): pl.pallas_call(kernel, out_shape=jax.ShapeDtypeStruct((slab, width), jnp....  39.5 us
    unnamed x1, local copies, waits for them, and re-layouts  1.73 us

profile of v4, /device:TPU:0, one launch (start us, length us, event | category | flops | bytes accessed | tf_op | source)
XLA Modules:
  0.0 41.2 jit_solution(2620139425047512226)
XLA Ops:
  0.0 39.5 %shard_map.46 = bf16[256,640]{1,0:T(8,128)(2,1)} custom-call(bf16[64,2560]{1,0:T(8,128)(2,1)} %lat.1, bf16[3,2560,640]{2,1,0:T(8,128)(2,1)} %bitcast.1, s32[4,4,4]{2,1,0:T(4,128)} %slots_hbm.1, s32[4,4]{1,0:T(4,128)} %count_hbm.1), custom_call_target="tpu_custom_call" | custom-call | tf_op jit(solution)/shard_map/pallas_call | solution.py:365
  39.5 1.7 %copy.6 = bf16[256,640]{1,0:T(8,128)(2,1)} copy(bf16[256,640]{1,0:T(8,128)(2,1)} %shard_map.46) | data formatting | bytes 655360

commit v5 on v4

--- a/solution.py
+++ b/solution.py
@@ -263,7 +263,6 @@
             arrived(slot)
         copy = copy_of(tokens.at[slot], slot, 13 + number, z, mate)
         copy.start()
-        arrived(b * 4 + (mate + 2) % 4)
         return [(copy, None)]
 
     inward = z + 1 - 2 * half
@@ -283,10 +282,16 @@
         part = jnp.dot(x, w[:, pl.ds(first, columns)], preferred_element_type=jnp.float32)
         store[...] = part.astype(jnp.bfloat16)
 
-    def attend(b, place, length, first):
+    def whole(b):
+        arrived(b * 4 + mate)
+        arrived(b * 4 + (mate + 2) % 4)
+
+    def attend(b, place, length, first, between=None):
         span = length * rows
         for tile in range(2 * width // 256):
             project(b * 4 + place, span, tile * 256, 256, kv.at[pl.ds(0, span), pl.ds(tile * 256, 256)])
+        if between is not None:
+            between()
         lane_block = (lax.broadcasted_iota(jnp.int32, (1, span), 1) + place * rows) // key_rows
         shades = []
         for a in range(blocks):
@@ -329,24 +334,31 @@
     own_upper = upper_of(z, 17, inward)
     pl.when(outer)(own_upper.start)
     late.append((own_upper, outer))
-    arrived(z * 4 + mate)
+    whole(z)
     for copy in local + w_copies:
         copy.wait()
     project(z * 4, slab, 2 * width, width, q)
-    attend(z, 0, 4, True)
-    forward(1, outer)
-    late += forward(2, middle)
-    late += pass_upper(others[0], 18, inward)
-    late += complete(1, others[0])
-    arrived(others[0] * 4 + mate)
-    attend(others[0], 0, 4, False)
-    forward(2, outer)
-    late += pass_upper(others[2], 19, z - 1 + 2 * half)
-    late += complete(2, others[1])
-    arrived(others[1] * 4 + mate)
-    attend(others[1], 0, 4, False)
-    arrived(others[2] * 4 + mate)
-    late += complete(3, others[2])
+
+    def pass_first():
+        forward(1, outer)
+        late.extend(forward(2, middle))
+        late.extend(pass_upper(others[0], 18, inward))
+        late.extend(complete(1, others[0]))
+
+    def pass_second():
+        forward(2, outer)
+        late.extend(pass_upper(others[2], 19, z - 1 + 2 * half))
+        late.extend(complete(2, others[1]))
+
+    def pass_third():
+        late.extend(complete(3, others[2]))
+
+    attend(z, 0, 4, True, pass_first)
+    whole(others[0])
+    attend(others[0], 0, 4, False, pass_second)
+    whole(others[1])
+    attend(others[1], 0, 4, False, pass_third)
+    whole(others[2])
     attend(others[2], 0, 4, False)
     for n in range(heads):
         out[:, pl.ds(n * HD, HD)] = (acc[n] / total[n]).astype(jnp.bfloat16)

time: 41.4 us -> 43 us (1.039)
  Pallas kernels: 39.5 us -> 41.1 us
    pallas_call x1, Pallas kernels: 39.5 us -> 41.1 us  [fused(): pl.pallas_call(kernel, out_shape=jax.ShapeDtypeStruct((slab, width), jnp....]
where the time goes in v5:
time: 43 us; the launch traced here: 42.8 us
  Pallas kernels  41.1 us (96%)
  local copies, waits for them, and re-layouts  1.73 us (4%)
    pallas_call x1, Pallas kernels, fused(): pl.pallas_call(kernel, out_shape=jax.ShapeDtypeStruct((slab, width), jnp....  41.1 us
    unnamed x1, local copies, waits for them, and re-layouts  1.73 us

profile of v5, /device:TPU:0, one launch (start us, length us, event | category | flops | bytes accessed | tf_op | source)
XLA Modules:
  0.0 42.8 jit_solution(9085030311100996940)
XLA Ops:
  0.0 41.1 %shard_map.46 = bf16[256,640]{1,0:T(8,128)(2,1)} custom-call(bf16[64,2560]{1,0:T(8,128)(2,1)} %lat.1, bf16[3,2560,640]{2,1,0:T(8,128)(2,1)} %bitcast.1, s32[4,4,4]{2,1,0:T(4,128)} %slots_hbm.1, s32[4,4]{1,0:T(4,128)} %count_hbm.1), custom_call_target="tpu_custom_call" | custom-call | tf_op jit(solution)/shard_map/pallas_call | solution.py:377
  41.1 1.7 %copy.6 = bf16[256,640]{1,0:T(8,128)(2,1)} copy(bf16[256,640]{1,0:T(8,128)(2,1)} %shard_map.46) | data formatting | bytes 655360
